TPU v7x, 32 devices: a whole 2x2x4 slice. The times are simulated.
32 devices in a mesh: groups: 2 (over x), region: 16 (over z, y, core).
Axes of the slice: x: 2, y: 2, z: 4, core: 2. Of those that a mesh axis runs over, the one named last changes fastest.
Arguments:
- obs_pos: float32 [512, 2, 256], P(('groups', 'region')), parts along dimension 0, may hold values from 0 to 230400, as said below
- obs_sigma: float32 [512, 256], P(('groups', 'region')), parts along dimension 0, may hold values from 0.5 to 1.2
- obs_error: float32 [512, 256], P(('groups', 'region')), parts along dimension 0, may hold values from 0.2 to 2
- innovation: float32 [512, 64, 256], P(('groups', 'region')), parts along dimension 0, may hold values from -6 to 6
- obs_count: int32 [512], P(('groups', 'region')), parts along dimension 0, may hold values from 1 to 256
- pair_list: int32 [2, 3072], P(None, ('groups', 'region')), parts along dimension 1, may hold values from 0 to 255, as said below
- pair_live: int32 [32], P(('groups', 'region')), parts along dimension 0, may hold values from 16 to 96
Outputs:
- solution: float32 [512, 64, 256], P(('groups', 'region')), parts along dimension 0
- residual: float32 [512, 64, 256], P(('groups', 'region')), parts along dimension 0
There are 2 independent parts, one for each index of `groups`. A program takes and returns all parts, laid end to end along the dimension named above; each array names one. Nothing has to cross between parts.
Inputs may be any that keep to these rules, and one draw needn't show every extreme that they name: `obs_pos`: block b's observations lie in cell b, an interval of the first coordinate 300 to 900 km long; cells follow one another without gaps in block order from 0; the second coordinate lies in 0 to 600 km. `pair_list`: device k's 96 slots hold pairs (i, j) with i among its 16 blocks and i <= j <= i + 5; its first pair_live[k] slots list, each once, every pair of such an i with a block j >= i whose cells lie less than 1500 km apart (i = j included); the other slots hold (k * 16, k * 16).
All inputs are finite; a program needn't handle non-finite values.
Results may differ from a plain program's by a relative error of at most 0.0003.
Values sent between devices are 32-bit elements; how exact they have to be, the bound alone decides.
No kernel may reach another device: no remote copies, remote signals or barrier semaphores. Data moves between devices by JAX's collectives and lax.ppermute only.
A program may use at most 64 MiB of HBM per device.

v0:
```python
import jax
import jax.numpy as jnp
from jax import lax
from jax.sharding import PartitionSpec as P

REACH = 5
ITERS = 2


CUTOFF_KM = 1500.0
SCALE_KM = 1000.0
pair_group = 12


def passed_along(block, axis, distance):
    devices = range(lax.axis_size(axis))
    route = [(i - distance, i) for i in devices if i - distance in devices]
    return lax.ppermute(block, axis, route)


def build_tiles(geo_first, geo_second):
    delta_x = geo_first[:, 0, :, None] - geo_second[:, 0, None, :]
    delta_y = geo_first[:, 1, :, None] - geo_second[:, 1, None, :]
    distance = jnp.sqrt(delta_x * delta_x + delta_y * delta_y)
    tapered = jnp.maximum(1.0 - distance / CUTOFF_KM, 0.0)
    return (
        geo_first[:, 2, :, None]
        * geo_second[:, 2, None, :]
        * (jnp.exp(-distance / SCALE_KM) * tapered * tapered)
    )


def pair_terms(geo_window, dir_window, first_loc, second_loc):
    pair_count = first_loc.shape[0]
    groups = pair_count // pair_group

    def group_terms(locations):
        first_part, second_part = locations
        tiles = build_tiles(
            jnp.take(geo_window, first_part, axis=0), jnp.take(geo_window, second_part, axis=0)
        )
        transposed = jnp.einsum(
            "pab,pma->pmb",
            tiles,
            jnp.take(dir_window, first_part, axis=0),
            precision=lax.Precision.HIGHEST,
        )
        forward_terms = jnp.einsum(
            "pab,pmb->pma",
            tiles,
            jnp.take(dir_window, second_part, axis=0),
            precision=lax.Precision.HIGHEST,
        )
        return (forward_terms, transposed)

    results = lax.map(
        group_terms, (first_loc.reshape(groups, pair_group), second_loc.reshape(groups, pair_group))
    )
    out_shape = (pair_count,) + dir_window.shape[1:]
    return tuple((entry.reshape(out_shape) for entry in results))


def collect(locations, weights, terms, window):
    one_hot = (locations[:, None] == jnp.arange(window, dtype=jnp.int32)[None, :]).astype(
        jnp.float32
    ) * weights[:, None]
    flat_terms = terms.reshape(terms.shape[0], -1)
    summed = jnp.einsum("pw,pk->wk", one_hot, flat_terms, precision=lax.Precision.HIGHEST)
    return summed.reshape((window,) + terms.shape[1:])


def member_sum(values):
    return jnp.sum(values, axis=(0, 2))


def squares(residual):
    return lax.psum(member_sum(residual * residual), "region")


def body(obs_pos, obs_sigma, obs_error, innovation, obs_count, pair_list, pair_live):
    blocks = obs_sigma.shape[0]
    obs_slots = obs_sigma.shape[1]
    first_block = lax.axis_index("region") * blocks
    obs_mask = (jnp.arange(obs_slots, dtype=jnp.int32)[None, :] < obs_count[:, None]).astype(
        jnp.float32
    )
    geometry = jnp.concatenate([obs_pos, (obs_sigma * obs_mask)[:, None, :]], axis=1)
    pair_total = pair_list.shape[1]
    slot_index = jnp.arange(pair_total, dtype=jnp.int32)
    own_live = slot_index < pair_live[0]
    error_rows = obs_error[:, None, :]
    geo_ahead = passed_along(geometry[:REACH], "region", -1)
    geo_window = jnp.concatenate([geometry, geo_ahead], axis=0)
    window = blocks + REACH
    first_loc = pair_list[0] - first_block
    second_loc = pair_list[1] - first_block
    forward_weight = own_live.astype(jnp.float32)
    transposed_weight = (own_live & (first_loc != second_loc)).astype(jnp.float32)
    residual = innovation * obs_mask[:, None, :]
    solution = jnp.zeros_like(residual)
    direction = residual
    norm_now = squares(residual)
    for iteration in range(ITERS):
        dir_ahead = passed_along(direction[:REACH], "region", -1)
        dir_window = jnp.concatenate([direction, dir_ahead], axis=0)
        forward_terms, transposed = pair_terms(geo_window, dir_window, first_loc, second_loc)
        window_sums = collect(first_loc, forward_weight, forward_terms, window) + collect(
            second_loc, transposed_weight, transposed, window
        )
        returned = passed_along(window_sums[blocks:], "region", 1)
        padding = jnp.zeros((blocks - REACH,) + returned.shape[1:], jnp.float32)
        own_rows = window_sums[:blocks] + jnp.concatenate([returned, padding], axis=0)
        image = own_rows + error_rows * direction
        alpha = norm_now / lax.psum(member_sum(direction * image), "region")
        solution = solution + alpha[None, :, None] * direction
        residual = residual - alpha[None, :, None] * image
        if iteration + 1 < ITERS:
            norm_next = squares(residual)
            direction = residual + (norm_next / norm_now)[None, :, None] * direction
            norm_now = norm_next
    return (solution, residual)


def solution(mesh):
    return jax.shard_map(
        body,
        mesh=mesh,
        in_specs=(
            P(("groups", "region"), None, None),
            P(("groups", "region"), None),
            P(("groups", "region"), None),
            P(("groups", "region"), None, None),
            P(("groups", "region")),
            P(None, ("groups", "region")),
            P(("groups", "region")),
        ),
        out_specs=(P(("groups", "region"), None, None), P(("groups", "region"), None, None)),
        check_vma=False,
    )
```

profile of v0, /device:TPU:0, one launch (start us, length us, event | category | flops | bytes accessed | tf_op | source)
XLA Modules:
  0.0 519.1 jit_solution(2048200632845827512)
XLA Ops:
  1.4 1.8 copy_multiply_fusion
  9.1 3.4 broadcast.112.clone
  12.6 3.4 broadcast.112.clone.1
  16.0 122.0 %while.24 = (s32[]{:T(128)}, f32[8,12,64,256]{3,2,1,0:T(8,128)}, f32[8,12,64,256]{3,2,1,0:T(8,128)}, s32[8,12]{1,0:T(8,128)}, f32[21,64,256]{2,1,0:T(8,128)S(1)}...) while((s32[]{:T(128)}, f32[8,12,64,256]{3,2,1,0:T(8,128)}, f32[8,12,64,256]{3,2,1,0:T(8,128)}, ...), condition=%wide.region_3.6_spmd, body=%wide.region_2.5_spmd.sunk | while | flops 1230393472 | bytes 7038593 | solution.py:56
  18.8 5.5 %fusion.187 = f32[8,12,64,256]{3,2,1,0:T(8,128)} fusion(f32[8,12,64,256]{3,2,1,0:T(8,128)} %get-tuple-element.318, s32[]{:T(128)} %get-tuple-element.316, f32[12,256]{1,0:T(8,128)S(1)} %bitcast.190, f32[12,256]{1,0:T(8,128)S(1)} %bitcast.178, f32[12,256]{1,0:T(8,128)S(1)} %bitcast.194, f32[12,256]{1,0:T(8,128)S(1)} %bitcast.182, ...), kind=kOutput, calls=%fused_computation.35.clone.1 | convolution fusion | flops 615186432 | bytes 1647116 | tf_op jit(solution)/shard_map/while/body/eval_jaxpr/pab,pma->pmb/dot_general | solution.py:42
  24.8 6.4 %fusion.186 = f32[8,12,64,256]{3,2,1,0:T(8,128)} fusion(f32[8,12,64,256]{3,2,1,0:T(8,128)} %get-tuple-element.317, s32[]{:T(128)} %get-tuple-element.316, f32[12,256]{1,0:T(8,128)S(1)} %bitcast.191, f32[12,256]{1,0:T(8,128)S(1)} %bitcast.179, f32[12,256]{1,0:T(8,128)S(1)} %bitcast.195, f32[12,256]{1,0:T(8,128)S(1)} %bitcast.183, ...), kind=kOutput, calls=%fused_computation.33.clone.1 | convolution fusion | flops 615186432 | bytes 1647116 | tf_op jit(solution)/shard_map/while/body/eval_jaxpr/pab,pmb->pma/dot_general | solution.py:48
  34.0 5.5 %fusion.187 = f32[8,12,64,256]{3,2,1,0:T(8,128)} fusion(f32[8,12,64,256]{3,2,1,0:T(8,128)} %get-tuple-element.318, s32[]{:T(128)} %get-tuple-element.316, f32[12,256]{1,0:T(8,128)S(1)} %bitcast.190, f32[12,256]{1,0:T(8,128)S(1)} %bitcast.178, f32[12,256]{1,0:T(8,128)S(1)} %bitcast.194, f32[12,256]{1,0:T(8,128)S(1)} %bitcast.182, ...), kind=kOutput, calls=%fused_computation.35.clone.1 | convolution fusion | flops 615186432 | bytes 1647116 | tf_op jit(solution)/shard_map/while/body/eval_jaxpr/pab,pma->pmb/dot_general | solution.py:42
  40.1 6.4 %fusion.186 = f32[8,12,64,256]{3,2,1,0:T(8,128)} fusion(f32[8,12,64,256]{3,2,1,0:T(8,128)} %get-tuple-element.317, s32[]{:T(128)} %get-tuple-element.316, f32[12,256]{1,0:T(8,128)S(1)} %bitcast.191, f32[12,256]{1,0:T(8,128)S(1)} %bitcast.179, f32[12,256]{1,0:T(8,128)S(1)} %bitcast.195, f32[12,256]{1,0:T(8,128)S(1)} %bitcast.183, ...), kind=kOutput, calls=%fused_computation.33.clone.1 | convolution fusion | flops 615186432 | bytes 1647116 | tf_op jit(solution)/shard_map/while/body/eval_jaxpr/pab,pmb->pma/dot_general | solution.py:48
  49.3 5.5 %fusion.187 = f32[8,12,64,256]{3,2,1,0:T(8,128)} fusion(f32[8,12,64,256]{3,2,1,0:T(8,128)} %get-tuple-element.318, s32[]{:T(128)} %get-tuple-element.316, f32[12,256]{1,0:T(8,128)S(1)} %bitcast.190, f32[12,256]{1,0:T(8,128)S(1)} %bitcast.178, f32[12,256]{1,0:T(8,128)S(1)} %bitcast.194, f32[12,256]{1,0:T(8,128)S(1)} %bitcast.182, ...), kind=kOutput, calls=%fused_computation.35.clone.1 | convolution fusion | flops 615186432 | bytes 1647116 | tf_op jit(solution)/shard_map/while/body/eval_jaxpr/pab,pma->pmb/dot_general | solution.py:42
  55.3 6.4 %fusion.186 = f32[8,12,64,256]{3,2,1,0:T(8,128)} fusion(f32[8,12,64,256]{3,2,1,0:T(8,128)} %get-tuple-element.317, s32[]{:T(128)} %get-tuple-element.316, f32[12,256]{1,0:T(8,128)S(1)} %bitcast.191, f32[12,256]{1,0:T(8,128)S(1)} %bitcast.179, f32[12,256]{1,0:T(8,128)S(1)} %bitcast.195, f32[12,256]{1,0:T(8,128)S(1)} %bitcast.183, ...), kind=kOutput, calls=%fused_computation.33.clone.1 | convolution fusion | flops 615186432 | bytes 1647116 | tf_op jit(solution)/shard_map/while/body/eval_jaxpr/pab,pmb->pma/dot_general | solution.py:48
  64.5 5.5 %fusion.187 = f32[8,12,64,256]{3,2,1,0:T(8,128)} fusion(f32[8,12,64,256]{3,2,1,0:T(8,128)} %get-tuple-element.318, s32[]{:T(128)} %get-tuple-element.316, f32[12,256]{1,0:T(8,128)S(1)} %bitcast.190, f32[12,256]{1,0:T(8,128)S(1)} %bitcast.178, f32[12,256]{1,0:T(8,128)S(1)} %bitcast.194, f32[12,256]{1,0:T(8,128)S(1)} %bitcast.182, ...), kind=kOutput, calls=%fused_computation.35.clone.1 | convolution fusion | flops 615186432 | bytes 1647116 | tf_op jit(solution)/shard_map/while/body/eval_jaxpr/pab,pma->pmb/dot_general | solution.py:42
  70.6 6.4 %fusion.186 = f32[8,12,64,256]{3,2,1,0:T(8,128)} fusion(f32[8,12,64,256]{3,2,1,0:T(8,128)} %get-tuple-element.317, s32[]{:T(128)} %get-tuple-element.316, f32[12,256]{1,0:T(8,128)S(1)} %bitcast.191, f32[12,256]{1,0:T(8,128)S(1)} %bitcast.179, f32[12,256]{1,0:T(8,128)S(1)} %bitcast.195, f32[12,256]{1,0:T(8,128)S(1)} %bitcast.183, ...), kind=kOutput, calls=%fused_computation.33.clone.1 | convolution fusion | flops 615186432 | bytes 1647116 | tf_op jit(solution)/shard_map/while/body/eval_jaxpr/pab,pmb->pma/dot_general | solution.py:48
  79.8 5.5 %fusion.187 = f32[8,12,64,256]{3,2,1,0:T(8,128)} fusion(f32[8,12,64,256]{3,2,1,0:T(8,128)} %get-tuple-element.318, s32[]{:T(128)} %get-tuple-element.316, f32[12,256]{1,0:T(8,128)S(1)} %bitcast.190, f32[12,256]{1,0:T(8,128)S(1)} %bitcast.178, f32[12,256]{1,0:T(8,128)S(1)} %bitcast.194, f32[12,256]{1,0:T(8,128)S(1)} %bitcast.182, ...), kind=kOutput, calls=%fused_computation.35.clone.1 | convolution fusion | flops 615186432 | bytes 1647116 | tf_op jit(solution)/shard_map/while/body/eval_jaxpr/pab,pma->pmb/dot_general | solution.py:42
  85.8 6.4 %fusion.186 = f32[8,12,64,256]{3,2,1,0:T(8,128)} fusion(f32[8,12,64,256]{3,2,1,0:T(8,128)} %get-tuple-element.317, s32[]{:T(128)} %get-tuple-element.316, f32[12,256]{1,0:T(8,128)S(1)} %bitcast.191, f32[12,256]{1,0:T(8,128)S(1)} %bitcast.179, f32[12,256]{1,0:T(8,128)S(1)} %bitcast.195, f32[12,256]{1,0:T(8,128)S(1)} %bitcast.183, ...), kind=kOutput, calls=%fused_computation.33.clone.1 | convolution fusion | flops 615186432 | bytes 1647116 | tf_op jit(solution)/shard_map/while/body/eval_jaxpr/pab,pmb->pma/dot_general | solution.py:48
  95.0 5.5 %fusion.187 = f32[8,12,64,256]{3,2,1,0:T(8,128)} fusion(f32[8,12,64,256]{3,2,1,0:T(8,128)} %get-tuple-element.318, s32[]{:T(128)} %get-tuple-element.316, f32[12,256]{1,0:T(8,128)S(1)} %bitcast.190, f32[12,256]{1,0:T(8,128)S(1)} %bitcast.178, f32[12,256]{1,0:T(8,128)S(1)} %bitcast.194, f32[12,256]{1,0:T(8,128)S(1)} %bitcast.182, ...), kind=kOutput, calls=%fused_computation.35.clone.1 | convolution fusion | flops 615186432 | bytes 1647116 | tf_op jit(solution)/shard_map/while/body/eval_jaxpr/pab,pma->pmb/dot_general | solution.py:42
  101.1 6.4 %fusion.186 = f32[8,12,64,256]{3,2,1,0:T(8,128)} fusion(f32[8,12,64,256]{3,2,1,0:T(8,128)} %get-tuple-element.317, s32[]{:T(128)} %get-tuple-element.316, f32[12,256]{1,0:T(8,128)S(1)} %bitcast.191, f32[12,256]{1,0:T(8,128)S(1)} %bitcast.179, f32[12,256]{1,0:T(8,128)S(1)} %bitcast.195, f32[12,256]{1,0:T(8,128)S(1)} %bitcast.183, ...), kind=kOutput, calls=%fused_computation.33.clone.1 | convolution fusion | flops 615186432 | bytes 1647116 | tf_op jit(solution)/shard_map/while/body/eval_jaxpr/pab,pmb->pma/dot_general | solution.py:48
  110.3 5.5 %fusion.187 = f32[8,12,64,256]{3,2,1,0:T(8,128)} fusion(f32[8,12,64,256]{3,2,1,0:T(8,128)} %get-tuple-element.318, s32[]{:T(128)} %get-tuple-element.316, f32[12,256]{1,0:T(8,128)S(1)} %bitcast.190, f32[12,256]{1,0:T(8,128)S(1)} %bitcast.178, f32[12,256]{1,0:T(8,128)S(1)} %bitcast.194, f32[12,256]{1,0:T(8,128)S(1)} %bitcast.182, ...), kind=kOutput, calls=%fused_computation.35.clone.1 | convolution fusion | flops 615186432 | bytes 1647116 | tf_op jit(solution)/shard_map/while/body/eval_jaxpr/pab,pma->pmb/dot_general | solution.py:42
  116.3 6.4 %fusion.186 = f32[8,12,64,256]{3,2,1,0:T(8,128)} fusion(f32[8,12,64,256]{3,2,1,0:T(8,128)} %get-tuple-element.317, s32[]{:T(128)} %get-tuple-element.316, f32[12,256]{1,0:T(8,128)S(1)} %bitcast.191, f32[12,256]{1,0:T(8,128)S(1)} %bitcast.179, f32[12,256]{1,0:T(8,128)S(1)} %bitcast.195, f32[12,256]{1,0:T(8,128)S(1)} %bitcast.183, ...), kind=kOutput, calls=%fused_computation.33.clone.1 | convolution fusion | flops 615186432 | bytes 1647116 | tf_op jit(solution)/shard_map/while/body/eval_jaxpr/pab,pmb->pma/dot_general | solution.py:48
  125.5 5.5 %fusion.187 = f32[8,12,64,256]{3,2,1,0:T(8,128)} fusion(f32[8,12,64,256]{3,2,1,0:T(8,128)} %get-tuple-element.318, s32[]{:T(128)} %get-tuple-element.316, f32[12,256]{1,0:T(8,128)S(1)} %bitcast.190, f32[12,256]{1,0:T(8,128)S(1)} %bitcast.178, f32[12,256]{1,0:T(8,128)S(1)} %bitcast.194, f32[12,256]{1,0:T(8,128)S(1)} %bitcast.182, ...), kind=kOutput, calls=%fused_computation.35.clone.1 | convolution fusion | flops 615186432 | bytes 1647116 | tf_op jit(solution)/shard_map/while/body/eval_jaxpr/pab,pma->pmb/dot_general | solution.py:42
  131.6 6.4 %fusion.186 = f32[8,12,64,256]{3,2,1,0:T(8,128)} fusion(f32[8,12,64,256]{3,2,1,0:T(8,128)} %get-tuple-element.317, s32[]{:T(128)} %get-tuple-element.316, f32[12,256]{1,0:T(8,128)S(1)} %bitcast.191, f32[12,256]{1,0:T(8,128)S(1)} %bitcast.179, f32[12,256]{1,0:T(8,128)S(1)} %bitcast.195, f32[12,256]{1,0:T(8,128)S(1)} %bitcast.183, ...), kind=kOutput, calls=%fused_computation.33.clone.1 | convolution fusion | flops 615186432 | bytes 1647116 | tf_op jit(solution)/shard_map/while/body/eval_jaxpr/pab,pmb->pma/dot_general | solution.py:48
  138.0 9.9 %fusion.116 = f32[21,64,256]{2,0,1:T(8,128)S(1)} fusion(f32[96]{0:T(128)S(1)} %get-tuple-element.180, s32[96]{0:T(128)S(1)} %get-tuple-element.179, f32[12,8,64,256]{3,2,1,0:T(8,128)} %bitcast.177), kind=kOutput, calls=%fused_computation.138 | convolution fusion | flops 396365760 | bytes 7668480 | tf_op jit(solution)/shard_map/pw,pk->wk/dot_general | solution.py:68
  147.9 6.6 %fusion.122 = f32[21,64,256]{2,0,1:T(8,128)S(1)} fusion(f32[21,64,256]{2,0,1:T(8,128)S(1)} %fusion.116, f32[96]{0:T(128)S(1)} %get-tuple-element.181, s32[96]{0:T(128)S(1)} %get-tuple-element.178, f32[12,8,64,256]{3,2,1,0:T(8,128)S(1)} %bitcast.176), kind=kOutput, calls=%fused_computation.146 | convolution fusion | flops 396709824 | bytes 9044736 | tf_op jit(solution)/shard_map/pw,pk->wk/dot_general | solution.py:68
  154.5 8.9 %collective-permute-start.2 = (f32[5,64,256]{2,0,1:T(8,128)S(1)}, f32[5,64,256]{2,0,1:T(8,128)S(1)}, u32[]{:S(2)}, u32[]{:S(2)}) collective-permute-start(f32[5,64,256]{2,0,1:T(8,128)S(1)} %slice.102), channel_id=1, source_target_pairs={{0,1},{1,2},{2,3},{3,4},{4,5},{5,6},{6,7},{7,8},{8,9},{9,10},{10,1... | collective-permute-start | bytes 983048 | tf_op jit(solution)/shard_map/ppermute | solution.py:18
  165.7 34.7 %all-reduce.2 = (f32[64]{0:T(128)S(1)}, f32[64]{0:T(128)S(1)}) all-reduce(f32[64]{0:T(128)S(1)} %get-tuple-element.117, f32[64]{0:T(128)S(1)} %get-tuple-element.116), channel_id=1, replica_groups=mesh['groups'=2,'region'=16] {'region'}, use_global_device_ids=true, to_apply=%region_1.0 | all-reduce | flops 128 | bytes 1024 | tf_op jit(solution)/shard_map/psum | solution.py:77
  200.4 2.2 multiply_reduce_fusion.1
  202.7 29.8 %psum.30 = f32[64]{0:T(128)S(1)} all-reduce(f32[64]{0:T(128)S(1)} %get-tuple-element.158), channel_id=1, replica_groups=mesh['groups'=2,'region'=16] {'region'}, use_global_device_ids=true, to_apply=%region_7.10 | all-reduce | flops 64 | bytes 512 | tf_op jit(solution)/shard_map/psum | solution.py:77
  234.5 2.5 collective-permute-done.3
  237.6 3.4 broadcast.112
  241.1 3.4 broadcast.112.clone.2
  244.4 206.8 %while.25 = (s32[]{:T(128)}, f32[8,12,64,256]{3,2,1,0:T(8,128)}, f32[8,12,64,256]{3,2,1,0:T(8,128)}, s32[8,12]{1,0:T(8,128)}, f32[21,64,256]{2,1,0:T(8,128)S(1)}...) while((s32[]{:T(128)}, f32[8,12,64,256]{3,2,1,0:T(8,128)}, f32[8,12,64,256]{3,2,1,0:T(8,128)}, ...), condition=%wide.region_9.12_spmd, body=%wide.region_8.11_spmd.sunk | while | flops 1230393472 | bytes 7179017 | solution.py:56
  253.5 1.6 gather_fusion.7
  255.1 6.5 %fusion.195 = f32[8,12,64,256]{3,2,1,0:T(8,128)} fusion(f32[8,12,64,256]{3,2,1,0:T(8,128)} %get-tuple-element.342, s32[]{:T(128)} %get-tuple-element.340, f32[12,256]{1,0:T(8,128)S(1)} %bitcast.192, f32[12,256]{1,0:T(8,128)S(1)} %bitcast.180, f32[12,256]{1,0:T(8,128)} %bitcast.196, f32[12,256]{1,0:T(8,128)} %bitcast.184, f32[12,256]{1,0:T(8,128)} %bitcast.200, ...), kind=kOutput, calls=%fused_computation.97.clone.1 | convolution fusion | flops 615186432 | bytes 1664000 | tf_op jit(solution)/shard_map/while/body/eval_jaxpr/pab,pma->pmb/dot_general | solution.py:42
  261.6 1.6 gather_fusion.6
  263.2 7.3 %fusion.194 = f32[8,12,64,256]{3,2,1,0:T(8,128)} fusion(f32[8,12,64,256]{3,2,1,0:T(8,128)} %get-tuple-element.341, s32[]{:T(128)} %get-tuple-element.340, f32[12,256]{1,0:T(8,128)S(1)} %bitcast.193, f32[12,256]{1,0:T(8,128)S(1)} %bitcast.181, f32[12,256]{1,0:T(8,128)} %bitcast.197, f32[12,256]{1,0:T(8,128)S(1)} %bitcast.185, ...), kind=kOutput, calls=%fused_computation.95.clone.1 | convolution fusion | flops 615186432 | bytes 1655808 | tf_op jit(solution)/shard_map/while/body/eval_jaxpr/pab,pmb->pma/dot_general | solution.py:48
  279.3 1.6 gather_fusion.7
  280.9 6.5 %fusion.195 = f32[8,12,64,256]{3,2,1,0:T(8,128)} fusion(f32[8,12,64,256]{3,2,1,0:T(8,128)} %get-tuple-element.342, s32[]{:T(128)} %get-tuple-element.340, f32[12,256]{1,0:T(8,128)S(1)} %bitcast.192, f32[12,256]{1,0:T(8,128)S(1)} %bitcast.180, f32[12,256]{1,0:T(8,128)} %bitcast.196, f32[12,256]{1,0:T(8,128)} %bitcast.184, f32[12,256]{1,0:T(8,128)} %bitcast.200, ...), kind=kOutput, calls=%fused_computation.97.clone.1 | convolution fusion | flops 615186432 | bytes 1664000 | tf_op jit(solution)/shard_map/while/body/eval_jaxpr/pab,pma->pmb/dot_general | solution.py:42
  287.4 1.6 gather_fusion.6
  289.0 7.3 %fusion.194 = f32[8,12,64,256]{3,2,1,0:T(8,128)} fusion(f32[8,12,64,256]{3,2,1,0:T(8,128)} %get-tuple-element.341, s32[]{:T(128)} %get-tuple-element.340, f32[12,256]{1,0:T(8,128)S(1)} %bitcast.193, f32[12,256]{1,0:T(8,128)S(1)} %bitcast.181, f32[12,256]{1,0:T(8,128)} %bitcast.197, f32[12,256]{1,0:T(8,128)S(1)} %bitcast.185, ...), kind=kOutput, calls=%fused_computation.95.clone.1 | convolution fusion | flops 615186432 | bytes 1655808 | tf_op jit(solution)/shard_map/while/body/eval_jaxpr/pab,pmb->pma/dot_general | solution.py:48
  305.1 1.6 gather_fusion.7
  306.7 6.5 %fusion.195 = f32[8,12,64,256]{3,2,1,0:T(8,128)} fusion(f32[8,12,64,256]{3,2,1,0:T(8,128)} %get-tuple-element.342, s32[]{:T(128)} %get-tuple-element.340, f32[12,256]{1,0:T(8,128)S(1)} %bitcast.192, f32[12,256]{1,0:T(8,128)S(1)} %bitcast.180, f32[12,256]{1,0:T(8,128)} %bitcast.196, f32[12,256]{1,0:T(8,128)} %bitcast.184, f32[12,256]{1,0:T(8,128)} %bitcast.200, ...), kind=kOutput, calls=%fused_computation.97.clone.1 | convolution fusion | flops 615186432 | bytes 1664000 | tf_op jit(solution)/shard_map/while/body/eval_jaxpr/pab,pma->pmb/dot_general | solution.py:42
  313.2 1.6 gather_fusion.6
  314.8 7.3 %fusion.194 = f32[8,12,64,256]{3,2,1,0:T(8,128)} fusion(f32[8,12,64,256]{3,2,1,0:T(8,128)} %get-tuple-element.341, s32[]{:T(128)} %get-tuple-element.340, f32[12,256]{1,0:T(8,128)S(1)} %bitcast.193, f32[12,256]{1,0:T(8,128)S(1)} %bitcast.181, f32[12,256]{1,0:T(8,128)} %bitcast.197, f32[12,256]{1,0:T(8,128)S(1)} %bitcast.185, ...), kind=kOutput, calls=%fused_computation.95.clone.1 | convolution fusion | flops 615186432 | bytes 1655808 | tf_op jit(solution)/shard_map/while/body/eval_jaxpr/pab,pmb->pma/dot_general | solution.py:48
  332.6 6.5 %fusion.195 = f32[8,12,64,256]{3,2,1,0:T(8,128)} fusion(f32[8,12,64,256]{3,2,1,0:T(8,128)} %get-tuple-element.342, s32[]{:T(128)} %get-tuple-element.340, f32[12,256]{1,0:T(8,128)S(1)} %bitcast.192, f32[12,256]{1,0:T(8,128)S(1)} %bitcast.180, f32[12,256]{1,0:T(8,128)} %bitcast.196, f32[12,256]{1,0:T(8,128)} %bitcast.184, f32[12,256]{1,0:T(8,128)} %bitcast.200, ...), kind=kOutput, calls=%fused_computation.97.clone.1 | convolution fusion | flops 615186432 | bytes 1664000 | tf_op jit(solution)/shard_map/while/body/eval_jaxpr/pab,pma->pmb/dot_general | solution.py:42
  339.0 1.6 gather_fusion.6
  340.6 7.3 %fusion.194 = f32[8,12,64,256]{3,2,1,0:T(8,128)} fusion(f32[8,12,64,256]{3,2,1,0:T(8,128)} %get-tuple-element.341, s32[]{:T(128)} %get-tuple-element.340, f32[12,256]{1,0:T(8,128)S(1)} %bitcast.193, f32[12,256]{1,0:T(8,128)S(1)} %bitcast.181, f32[12,256]{1,0:T(8,128)} %bitcast.197, f32[12,256]{1,0:T(8,128)S(1)} %bitcast.185, ...), kind=kOutput, calls=%fused_computation.95.clone.1 | convolution fusion | flops 615186432 | bytes 1655808 | tf_op jit(solution)/shard_map/while/body/eval_jaxpr/pab,pmb->pma/dot_general | solution.py:48
  356.8 1.6 gather_fusion.7
  358.4 6.5 %fusion.195 = f32[8,12,64,256]{3,2,1,0:T(8,128)} fusion(f32[8,12,64,256]{3,2,1,0:T(8,128)} %get-tuple-element.342, s32[]{:T(128)} %get-tuple-element.340, f32[12,256]{1,0:T(8,128)S(1)} %bitcast.192, f32[12,256]{1,0:T(8,128)S(1)} %bitcast.180, f32[12,256]{1,0:T(8,128)} %bitcast.196, f32[12,256]{1,0:T(8,128)} %bitcast.184, f32[12,256]{1,0:T(8,128)} %bitcast.200, ...), kind=kOutput, calls=%fused_computation.97.clone.1 | convolution fusion | flops 615186432 | bytes 1664000 | tf_op jit(solution)/shard_map/while/body/eval_jaxpr/pab,pma->pmb/dot_general | solution.py:42
  364.9 1.6 gather_fusion.6
  366.5 7.3 %fusion.194 = f32[8,12,64,256]{3,2,1,0:T(8,128)} fusion(f32[8,12,64,256]{3,2,1,0:T(8,128)} %get-tuple-element.341, s32[]{:T(128)} %get-tuple-element.340, f32[12,256]{1,0:T(8,128)S(1)} %bitcast.193, f32[12,256]{1,0:T(8,128)S(1)} %bitcast.181, f32[12,256]{1,0:T(8,128)} %bitcast.197, f32[12,256]{1,0:T(8,128)S(1)} %bitcast.185, ...), kind=kOutput, calls=%fused_computation.95.clone.1 | convolution fusion | flops 615186432 | bytes 1655808 | tf_op jit(solution)/shard_map/while/body/eval_jaxpr/pab,pmb->pma/dot_general | solution.py:48
  382.6 1.6 gather_fusion.7
  384.2 6.5 %fusion.195 = f32[8,12,64,256]{3,2,1,0:T(8,128)} fusion(f32[8,12,64,256]{3,2,1,0:T(8,128)} %get-tuple-element.342, s32[]{:T(128)} %get-tuple-element.340, f32[12,256]{1,0:T(8,128)S(1)} %bitcast.192, f32[12,256]{1,0:T(8,128)S(1)} %bitcast.180, f32[12,256]{1,0:T(8,128)} %bitcast.196, f32[12,256]{1,0:T(8,128)} %bitcast.184, f32[12,256]{1,0:T(8,128)} %bitcast.200, ...), kind=kOutput, calls=%fused_computation.97.clone.1 | convolution fusion | flops 615186432 | bytes 1664000 | tf_op jit(solution)/shard_map/while/body/eval_jaxpr/pab,pma->pmb/dot_general | solution.py:42
  392.3 7.3 %fusion.194 = f32[8,12,64,256]{3,2,1,0:T(8,128)} fusion(f32[8,12,64,256]{3,2,1,0:T(8,128)} %get-tuple-element.341, s32[]{:T(128)} %get-tuple-element.340, f32[12,256]{1,0:T(8,128)S(1)} %bitcast.193, f32[12,256]{1,0:T(8,128)S(1)} %bitcast.181, f32[12,256]{1,0:T(8,128)} %bitcast.197, f32[12,256]{1,0:T(8,128)S(1)} %bitcast.185, ...), kind=kOutput, calls=%fused_computation.95.clone.1 | convolution fusion | flops 615186432 | bytes 1655808 | tf_op jit(solution)/shard_map/while/body/eval_jaxpr/pab,pmb->pma/dot_general | solution.py:48
  408.4 1.6 gather_fusion.7
  410.0 6.4 %fusion.195 = f32[8,12,64,256]{3,2,1,0:T(8,128)} fusion(f32[8,12,64,256]{3,2,1,0:T(8,128)} %get-tuple-element.342, s32[]{:T(128)} %get-tuple-element.340, f32[12,256]{1,0:T(8,128)S(1)} %bitcast.192, f32[12,256]{1,0:T(8,128)S(1)} %bitcast.180, f32[12,256]{1,0:T(8,128)} %bitcast.196, f32[12,256]{1,0:T(8,128)} %bitcast.184, f32[12,256]{1,0:T(8,128)} %bitcast.200, ...), kind=kOutput, calls=%fused_computation.97.clone.1 | convolution fusion | flops 615186432 | bytes 1664000 | tf_op jit(solution)/shard_map/while/body/eval_jaxpr/pab,pma->pmb/dot_general | solution.py:42
  416.5 1.6 gather_fusion.6
  418.1 7.3 %fusion.194 = f32[8,12,64,256]{3,2,1,0:T(8,128)} fusion(f32[8,12,64,256]{3,2,1,0:T(8,128)} %get-tuple-element.341, s32[]{:T(128)} %get-tuple-element.340, f32[12,256]{1,0:T(8,128)S(1)} %bitcast.193, f32[12,256]{1,0:T(8,128)S(1)} %bitcast.181, f32[12,256]{1,0:T(8,128)} %bitcast.197, f32[12,256]{1,0:T(8,128)S(1)} %bitcast.185, ...), kind=kOutput, calls=%fused_computation.95.clone.1 | convolution fusion | flops 615186432 | bytes 1655808 | tf_op jit(solution)/shard_map/while/body/eval_jaxpr/pab,pmb->pma/dot_general | solution.py:48
  434.3 1.6 gather_fusion.7
  435.9 6.5 %fusion.195 = f32[8,12,64,256]{3,2,1,0:T(8,128)} fusion(f32[8,12,64,256]{3,2,1,0:T(8,128)} %get-tuple-element.342, s32[]{:T(128)} %get-tuple-element.340, f32[12,256]{1,0:T(8,128)S(1)} %bitcast.192, f32[12,256]{1,0:T(8,128)S(1)} %bitcast.180, f32[12,256]{1,0:T(8,128)} %bitcast.196, f32[12,256]{1,0:T(8,128)} %bitcast.184, f32[12,256]{1,0:T(8,128)} %bitcast.200, ...), kind=kOutput, calls=%fused_computation.97.clone.1 | convolution fusion | flops 615186432 | bytes 1664000 | tf_op jit(solution)/shard_map/while/body/eval_jaxpr/pab,pma->pmb/dot_general | solution.py:42
  444.0 7.3 %fusion.194 = f32[8,12,64,256]{3,2,1,0:T(8,128)} fusion(f32[8,12,64,256]{3,2,1,0:T(8,128)} %get-tuple-element.341, s32[]{:T(128)} %get-tuple-element.340, f32[12,256]{1,0:T(8,128)S(1)} %bitcast.193, f32[12,256]{1,0:T(8,128)S(1)} %bitcast.181, f32[12,256]{1,0:T(8,128)} %bitcast.197, f32[12,256]{1,0:T(8,128)S(1)} %bitcast.185, ...), kind=kOutput, calls=%fused_computation.95.clone.1 | convolution fusion | flops 615186432 | bytes 1655808 | tf_op jit(solution)/shard_map/while/body/eval_jaxpr/pab,pmb->pma/dot_general | solution.py:48
  451.3 10.0 %fusion.110 = f32[21,64,256]{2,0,1:T(8,128)S(1)} fusion(f32[96]{0:T(128)} %copy-done.22, s32[96]{0:T(128)} %copy-done.19, f32[12,8,64,256]{3,2,1,0:T(8,128)} %bitcast.175), kind=kOutput, calls=%fused_computation.132 | convolution fusion | flops 396365760 | bytes 7668480 | tf_op jit(solution)/shard_map/pw,pk->wk/dot_general | solution.py:68
  461.3 6.6 %fusion.125 = f32[21,64,256]{2,0,1:T(8,128)S(1)} fusion(f32[21,64,256]{2,0,1:T(8,128)S(1)} %fusion.110, f32[96]{0:T(128)S(1)} %copy-done.21, s32[96]{0:T(128)S(1)} %copy-done.18, f32[12,8,64,256]{3,2,1,0:T(8,128)S(1)} %bitcast.174), kind=kOutput, calls=%fused_computation.147 | convolution fusion | flops 396709824 | bytes 9044736 | tf_op jit(solution)/shard_map/pw,pk->wk/dot_general | solution.py:68
  468.0 8.4 %collective-permute-start.4 = (f32[5,64,256]{2,0,1:T(8,128)S(1)}, f32[5,64,256]{2,0,1:T(8,128)S(1)}, u32[]{:S(2)}, u32[]{:S(2)}) collective-permute-start(f32[5,64,256]{2,0,1:T(8,128)S(1)} %slice.105), channel_id=1, source_target_pairs={{0,1},{1,2},{2,3},{3,4},{4,5},{5,6},{6,7},{7,8},{8,9},{9,10},{10,1... | collective-permute-start | bytes 983048 | tf_op jit(solution)/shard_map/ppermute | solution.py:18
  479.3 34.1 %psum.31 = f32[64]{0:T(128)S(1)} all-reduce(f32[64]{0:T(128)S(1)} %multiply_reduce_fusion), channel_id=1, replica_groups=mesh['groups'=2,'region'=16] {'region'}, use_global_device_ids=true, to_apply=%region_11.14 | all-reduce | flops 64 | bytes 512 | tf_op jit(solution)/shard_map/psum | solution.py:114
  513.4 2.1 multiply_subtract_fusion
  (405 shorter events, 118.4 us)
Async XLA Ops:
  0.6 4.0 copy-start.26
  0.6 4.0 copy-start.16
  0.7 4.1 copy-start.14
  0.7 6.1 %copy-start.23 = (s32[2,96]{1,0:T(2,128)S(1)}, s32[2,96]{1,0:T(2,128)}, u32[]{:S(2)}) copy-start(s32[2,96]{1,0:T(2,128)} %param.20) | copy-start | bytes 2308
  3.3 5.2 %collective-permute-start = (f32[5,64,256]{2,0,1:T(8,128)S(1)}, f32[5,64,256]{2,0,1:T(8,128)S(1)}, u32[]{:S(2)}, u32[]{:S(2)}) collective-permute-start(f32[5,64,256]{2,0,1:T(8,128)S(1)} %slice.100), channel_id=1, source_target_pairs={{1,0},{2,1},{3,2},{4,3},{5,4},{6,5},{7,6},{8,7},{9,8},{10,9},{11,1... | collective-permute-start | bytes 983048 | tf_op jit(solution)/shard_map/ppermute | solution.py:18
  4.8 3.7 collective-permute-start.1
  6.7 131.2 %copy-start.22 = (f32[96]{0:T(128)}, f32[96]{0:T(128)S(1)}, u32[]{:S(2)}) copy-start(f32[96]{0:T(128)S(1)} %get-tuple-element.180) | copy-start | bytes 1156
  6.7 141.1 %copy-start.20 = (f32[96]{0:T(128)}, f32[96]{0:T(128)S(1)}, u32[]{:S(2)}) copy-start(f32[96]{0:T(128)S(1)} %get-tuple-element.181) | copy-start | bytes 1156
  6.8 131.2 %copy-start.19 = (s32[96]{0:T(128)}, s32[96]{0:T(128)S(1)}, u32[]{:S(2)}) copy-start(s32[96]{0:T(128)S(1)} %get-tuple-element.179) | copy-start | bytes 1156
  6.8 141.1 %copy-start.17 = (s32[96]{0:T(128)}, s32[96]{0:T(128)S(1)}, u32[]{:S(2)}) copy-start(s32[96]{0:T(128)S(1)} %get-tuple-element.178) | copy-start | bytes 1156
  137.9 9.9 %copy-start.3 = (f32[21,3,256]{2,1,0:T(4,128)}, f32[21,3,256]{2,1,0:T(4,128)S(1)}, u32[]{:S(2)}) copy-start(f32[21,3,256]{2,1,0:T(4,128)S(1)} %get-tuple-element.356) | copy-start | bytes 193540
  138.0 9.9 %copy-start.2 = (f32[8,12,64,256]{3,2,1,0:T(8,128)S(1)}, f32[8,12,64,256]{3,2,1,0:T(8,128)}, u32[]{:S(2)}) copy-start(f32[8,12,64,256]{3,2,1,0:T(8,128)} %get-tuple-element.80) | copy-start | bytes 18874372
  147.9 17.0 %copy-start = (f32[16,64,256]{2,1,0:T(8,128)S(1)}, f32[16,64,256]{2,1,0:T(8,128)}, u32[]{:S(2)}) copy-start(f32[16,64,256]{2,1,0:T(8,128)} %param.18) | copy-start | bytes 3145732
  147.9 17.0 %copy-start.11 = (f32[16,256]{1,0:T(8,128)S(1)}, f32[16,256]{1,0:T(8,128)}, u32[]{:S(2)}) copy-start(f32[16,256]{1,0:T(8,128)} %param.17) | copy-start | bytes 49156
  154.5 10.4 %copy-start.4 = (f32[21,64,256]{2,0,1:T(8,128)}, f32[21,64,256]{2,0,1:T(8,128)S(1)}, u32[]{:S(2)}) copy-start(f32[21,64,256]{2,0,1:T(8,128)S(1)} %fusion.122) | copy-start | bytes 4128772
  154.5 10.3 %collective-permute-start.2 = (f32[5,64,256]{2,0,1:T(8,128)S(1)}, f32[5,64,256]{2,0,1:T(8,128)S(1)}, u32[]{:S(2)}, u32[]{:S(2)}) collective-permute-start(f32[5,64,256]{2,0,1:T(8,128)S(1)} %slice.102), channel_id=1, source_target_pairs={{0,1},{1,2},{2,3},{3,4},{4,5},{5,6},{6,7},{7,8},{8,9},{9,10},{10,1... | collective-permute-start | bytes 983048 | tf_op jit(solution)/shard_map/ppermute | solution.py:18
  200.4 32.7 %copy-start.24 = (f32[64]{0:T(128)}, f32[64]{0:T(128)S(1)}, u32[]{:S(2)}) copy-start(f32[64]{0:T(128)S(1)} %div.21) | copy-start | bytes 772
  202.7 34.3 %copy-start.6 = (f32[16,64,256]{2,0,1:T(8,128)}, f32[16,64,256]{2,0,1:T(8,128)S(1)}, u32[]{:S(2)}) copy-start(f32[16,64,256]{2,0,1:T(8,128)S(1)} %get-tuple-element.159) | copy-start | bytes 3145732
  232.5 4.7 copy-start.27
  233.2 3.8 collective-permute-start.3
  245.9 1.6 copy-start.15
  245.9 1.6 copy-start.13
  255.1 8.1 %copy-start.9 = (f32[12,1,256]{2,0,1:T(8,128)S(1)}, f32[12,1,256]{2,0,1:T(8,128)}, u32[]{:S(2)}) copy-start(f32[12,1,256]{2,0,1:T(8,128)} %copy.129) | copy-start | bytes 36868 | tf_op jit(solution)/shard_map/while
  255.1 8.1 %copy-start.10 = (f32[12,1,256]{2,0,1:T(8,128)S(1)}, f32[12,1,256]{2,0,1:T(8,128)}, u32[]{:S(2)}) copy-start(f32[12,1,256]{2,0,1:T(8,128)} %copy.131) | copy-start | bytes 36868 | tf_op jit(solution)/shard_map/while
  271.7 1.6 copy-start.15
  271.7 1.6 copy-start.13
  280.9 8.1 %copy-start.9 = (f32[12,1,256]{2,0,1:T(8,128)S(1)}, f32[12,1,256]{2,0,1:T(8,128)}, u32[]{:S(2)}) copy-start(f32[12,1,256]{2,0,1:T(8,128)} %copy.129) | copy-start | bytes 36868 | tf_op jit(solution)/shard_map/while
  280.9 8.1 %copy-start.10 = (f32[12,1,256]{2,0,1:T(8,128)S(1)}, f32[12,1,256]{2,0,1:T(8,128)}, u32[]{:S(2)}) copy-start(f32[12,1,256]{2,0,1:T(8,128)} %copy.131) | copy-start | bytes 36868 | tf_op jit(solution)/shard_map/while
  297.5 1.6 copy-start.15
  297.5 1.6 copy-start.13
  306.7 8.1 %copy-start.9 = (f32[12,1,256]{2,0,1:T(8,128)S(1)}, f32[12,1,256]{2,0,1:T(8,128)}, u32[]{:S(2)}) copy-start(f32[12,1,256]{2,0,1:T(8,128)} %copy.129) | copy-start | bytes 36868 | tf_op jit(solution)/shard_map/while
  306.7 8.1 %copy-start.10 = (f32[12,1,256]{2,0,1:T(8,128)S(1)}, f32[12,1,256]{2,0,1:T(8,128)}, u32[]{:S(2)}) copy-start(f32[12,1,256]{2,0,1:T(8,128)} %copy.131) | copy-start | bytes 36868 | tf_op jit(solution)/shard_map/while
  323.3 1.6 copy-start.15
  323.3 1.6 copy-start.13
  332.6 8.1 %copy-start.9 = (f32[12,1,256]{2,0,1:T(8,128)S(1)}, f32[12,1,256]{2,0,1:T(8,128)}, u32[]{:S(2)}) copy-start(f32[12,1,256]{2,0,1:T(8,128)} %copy.129) | copy-start | bytes 36868 | tf_op jit(solution)/shard_map/while
  332.6 8.1 %copy-start.10 = (f32[12,1,256]{2,0,1:T(8,128)S(1)}, f32[12,1,256]{2,0,1:T(8,128)}, u32[]{:S(2)}) copy-start(f32[12,1,256]{2,0,1:T(8,128)} %copy.131) | copy-start | bytes 36868 | tf_op jit(solution)/shard_map/while
  349.2 1.6 copy-start.15
  349.2 1.6 copy-start.13
  358.4 8.1 %copy-start.9 = (f32[12,1,256]{2,0,1:T(8,128)S(1)}, f32[12,1,256]{2,0,1:T(8,128)}, u32[]{:S(2)}) copy-start(f32[12,1,256]{2,0,1:T(8,128)} %copy.129) | copy-start | bytes 36868 | tf_op jit(solution)/shard_map/while
  358.4 8.1 %copy-start.10 = (f32[12,1,256]{2,0,1:T(8,128)S(1)}, f32[12,1,256]{2,0,1:T(8,128)}, u32[]{:S(2)}) copy-start(f32[12,1,256]{2,0,1:T(8,128)} %copy.131) | copy-start | bytes 36868 | tf_op jit(solution)/shard_map/while
  375.0 1.6 copy-start.15
  375.0 1.6 copy-start.13
  384.2 8.1 %copy-start.9 = (f32[12,1,256]{2,0,1:T(8,128)S(1)}, f32[12,1,256]{2,0,1:T(8,128)}, u32[]{:S(2)}) copy-start(f32[12,1,256]{2,0,1:T(8,128)} %copy.129) | copy-start | bytes 36868 | tf_op jit(solution)/shard_map/while
  384.2 8.1 %copy-start.10 = (f32[12,1,256]{2,0,1:T(8,128)S(1)}, f32[12,1,256]{2,0,1:T(8,128)}, u32[]{:S(2)}) copy-start(f32[12,1,256]{2,0,1:T(8,128)} %copy.131) | copy-start | bytes 36868 | tf_op jit(solution)/shard_map/while
  400.8 1.6 copy-start.15
  400.8 1.6 copy-start.13
  410.0 8.1 %copy-start.9 = (f32[12,1,256]{2,0,1:T(8,128)S(1)}, f32[12,1,256]{2,0,1:T(8,128)}, u32[]{:S(2)}) copy-start(f32[12,1,256]{2,0,1:T(8,128)} %copy.129) | copy-start | bytes 36868 | tf_op jit(solution)/shard_map/while
  410.0 8.1 %copy-start.10 = (f32[12,1,256]{2,0,1:T(8,128)S(1)}, f32[12,1,256]{2,0,1:T(8,128)}, u32[]{:S(2)}) copy-start(f32[12,1,256]{2,0,1:T(8,128)} %copy.131) | copy-start | bytes 36868 | tf_op jit(solution)/shard_map/while
  426.6 1.6 copy-start.15
  426.6 1.6 copy-start.13
  435.9 8.1 %copy-start.9 = (f32[12,1,256]{2,0,1:T(8,128)S(1)}, f32[12,1,256]{2,0,1:T(8,128)}, u32[]{:S(2)}) copy-start(f32[12,1,256]{2,0,1:T(8,128)} %copy.129) | copy-start | bytes 36868 | tf_op jit(solution)/shard_map/while
  435.9 8.1 %copy-start.10 = (f32[12,1,256]{2,0,1:T(8,128)S(1)}, f32[12,1,256]{2,0,1:T(8,128)}, u32[]{:S(2)}) copy-start(f32[12,1,256]{2,0,1:T(8,128)} %copy.131) | copy-start | bytes 36868 | tf_op jit(solution)/shard_map/while
  451.3 10.0 %copy-start.1 = (f32[8,12,64,256]{3,2,1,0:T(8,128)S(1)}, f32[8,12,64,256]{3,2,1,0:T(8,128)}, u32[]{:S(2)}) copy-start(f32[8,12,64,256]{3,2,1,0:T(8,128)} %get-tuple-element.82) | copy-start | bytes 18874372
  451.3 10.0 %copy-start.18 = (s32[96]{0:T(128)S(1)}, s32[96]{0:T(128)}, u32[]{:S(2)}) copy-start(s32[96]{0:T(128)} %copy-done.17) | copy-start | bytes 1156
  451.3 10.0 %copy-start.21 = (f32[96]{0:T(128)S(1)}, f32[96]{0:T(128)}, u32[]{:S(2)}) copy-start(f32[96]{0:T(128)} %copy-done.20) | copy-start | bytes 1156
  461.3 17.4 %copy-start.12 = (f32[16,256]{1,0:T(8,128)S(1)}, f32[16,256]{1,0:T(8,128)}, u32[]{:S(2)}) copy-start(f32[16,256]{1,0:T(8,128)} %param.17) | copy-start | bytes 49156
  467.9 10.0 %copy-start.5 = (f32[21,64,256]{2,0,1:T(8,128)}, f32[21,64,256]{2,0,1:T(8,128)S(1)}, u32[]{:S(2)}) copy-start(f32[21,64,256]{2,0,1:T(8,128)S(1)} %fusion.125) | copy-start | bytes 4128772
  467.9 45.5 %copy-start.28 = (f32[64]{0:T(128)S(1)}, f32[64]{0:T(128)}, u32[]{:S(2)}) copy-start(f32[64]{0:T(128)} %copy-done.27) | copy-start | bytes 772
  467.9 45.5 %copy-start.7 = (f32[16,64,256]{2,0,1:T(8,128)S(1)}, f32[16,64,256]{2,0,1:T(8,128)}, u32[]{:S(2)}) copy-start(f32[16,64,256]{2,0,1:T(8,128)} %copy-done.6) | copy-start | bytes 3145732
  467.9 45.5 %copy-start.25 = (f32[64]{0:T(128)S(1)}, f32[64]{0:T(128)}, u32[]{:S(2)}) copy-start(f32[64]{0:T(128)} %copy-done.24) | copy-start | bytes 772
  468.0 9.9 %collective-permute-start.4 = (f32[5,64,256]{2,0,1:T(8,128)S(1)}, f32[5,64,256]{2,0,1:T(8,128)S(1)}, u32[]{:S(2)}, u32[]{:S(2)}) collective-permute-start(f32[5,64,256]{2,0,1:T(8,128)S(1)} %slice.105), channel_id=1, source_target_pairs={{0,1},{1,2},{2,3},{3,4},{4,5},{5,6},{6,7},{7,8},{8,9},{9,10},{10,1... | collective-permute-start | bytes 983048 | tf_op jit(solution)/shard_map/ppermute | solution.py:18
  477.9 0.8 copy-start.8
where the time goes:
time: 528 us; the launch traced here: 519 us
  matrix products  238 us (45%)
  local copies, waits for them, and re-layouts  110 us (21%)
  blocking collectives  98.6 us (19%)
  other arithmetic  42.3 us (8%)
  starting transfers between devices  21.2 us (4%)
  waiting for transfers between devices  5.82 us (1%)
    dot_general x16, matrix products, group_terms(): jnp.einsum('pab,pmb->pma', tiles, jnp.take(dir_window, second_part, axis=...  109 us
    dot_general x16, matrix products, group_terms(): jnp.einsum('pab,pma->pmb', tiles, jnp.take(dir_window, first_part, axis=0...  95.4 us
    psum x2, blocking collectives, squares(): return lax.psum(member_sum(residual * residual), 'region')  64.5 us
    psum x1, blocking collectives, body(): alpha = norm_now / lax.psum(member_sum(direction * image), 'region')  34.1 us
    dot_general x4, matrix products, collect(): jnp.einsum('pw,pk->wk', one_hot, flat_terms, precision=lax.Precision.HIGH...  33 us
    ppermute x5, starting transfers between devices, passed_along(): return lax.ppermute(block, axis, route)  21.2 us
    while x160, local copies, waits for them, and re-layouts  19.6 us
    gather x16, local copies, waits for them, and re-layouts, group_terms(): jnp.take(dir_window, first_part, axis=0)  17.6 us
  transfers between devices with their start and end apart: 5, of which 4 were waited for; matrix products, arithmetic and copies ran while one was open for 0% of the time, Pallas kernels for 0%

commit v1 on v0

v1 whole, which is shorter than its diff:
```python
import functools

import jax
import jax.numpy as jnp
from jax import lax
from jax.experimental import pallas as pl
from jax.experimental.pallas import tpu as pltpu
from jax.sharding import PartitionSpec as P

REACH = 5
CUTOFF_KM = 1500.0
SCALE_KM = 1000.0
LOG2E = 1.4426950408889634
UNIT = LOG2E / SCALE_KM
TAPER = 1.0 / (CUTOFF_KM * UNIT)
LIMIT = CUTOFF_KM * UNIT
CH = 256
LN = 128
SPAN = 7
TINY = 1e-30
F32, BF16, I32 = jnp.float32, jnp.bfloat16, jnp.int32
VM = pl.BlockSpec(memory_space=pltpu.VMEM)
SM = pl.BlockSpec(memory_space=pltpu.SMEM)
HB = pl.BlockSpec(memory_space=pltpu.HBM)
MB = 1 << 20


def lanes(shape):
    return lax.broadcasted_iota(I32, shape, len(shape) - 1)


def at(start, size=CH):
    return pl.ds(pl.multiple_of(start, LN), size)


def pack_block(rows, count, offset, dst):
    base = (offset // LN) * LN
    shift = offset - base
    lane = lanes((rows.shape[0], LN))
    low = pltpu.roll(jnp.where(lane < count, rows[:, :LN], 0.0), shift, 1)
    high = pltpu.roll(jnp.where(lane + LN < count, rows[:, LN:], 0.0), shift, 1)
    before = lane < shift
    dst[:, at(base, LN)] = jnp.where(before, dst[:, at(base, LN)], low)
    dst[:, at(base + LN, LN)] = jnp.where(before, low, high)
    dst[:, at(base + 2 * LN, LN)] = jnp.where(before, high, 0.0)
    dst[:, at(base + 3 * LN, LN)] = jnp.zeros_like(low)


def split(values):
    high = values.astype(BF16)
    return high, (values - high.astype(F32)).astype(BF16)


def put_split(values, dst, place):
    high, low = split(values)
    half = values.shape[0]
    dst[place, :half, :] = high
    dst[place, half:, :] = low


def columns(row):
    parts = [jnp.broadcast_to(row[:, k : k + LN], (LN, LN)).T for k in (0, LN)]
    return jnp.concatenate(parts, axis=0)


def build(col_x, col_y, place, row_x, row_y, tile_ref, slot):
    strip = 32
    for top in range(0, CH, strip):
        for left in range(0, CH, LN):
            dx = col_x[place, top : top + strip, :] - row_x[:, left : left + LN]
            dy = col_y[place, top : top + strip, :] - row_y[:, left : left + LN]
            square = jnp.maximum(dx * dx + dy * dy, TINY)
            distance = square * lax.rsqrt(square)
            tapered = jnp.maximum(1.0 - distance * TAPER, 0.0)
            value = jnp.exp2(-distance) * (tapered * tapered)
            high, low = split(value)
            tile_ref[slot, top : top + strip, left : left + LN] = high
            tile_ref[slot, CH + top : CH + top + strip, left : left + LN] = low


def product(parts_ref, place, tile_ref, slot, transposed):
    dims = (((1,), (1 if transposed else 0,)), ((), ()))
    both = parts_ref[place]
    half = both.shape[0] // 2
    wide = lax.dot_general(both, tile_ref[slot, :CH, :], dims, preferred_element_type=F32)
    fine = lax.dot_general(both[:half], tile_ref[slot, CH:, :], dims, preferred_element_type=F32)
    return wide[:half] + wide[half:] + fine


def own_product(t, total, down, across, parts_ref, tile_ref, slot, acc):
    i, j = down[t], across[t]
    here = (t < total).astype(F32)
    other = jnp.where((t < total) & (i != j), 1.0, 0.0).astype(F32)
    forward = product(parts_ref, i, tile_ref, slot, False)
    backward = product(parts_ref, j, tile_ref, slot, True)
    acc[:, at(j * CH)] += here * forward
    acc[:, at(i * CH)] += other * backward


def edge_product(t, total, down, across, parts_ref, tile_ref, slot, acc):
    here = (t < total).astype(F32)
    acc[:, at(across[t] * CH)] += here * product(parts_ref, down[t], tile_ref, slot, False)


def fetch(pairs, sems):
    copies = [pltpu.make_async_copy(src, dst, sems.at[k]) for k, (src, dst) in enumerate(pairs)]
    for copy in copies:
        copy.start()
    for copy in copies:
        copy.wait()


def pack_sides(innov, pos_in, sigma_in, count_in, to_prev, to_next, pos, sigma, count, sems):
    blocks, members = innov.shape[0], innov.shape[1]
    ends = ((0, to_prev), (blocks - REACH, to_next))
    pairs = [(pos_in, pos), (sigma_in, sigma), (count_in, count)]
    for first, dst in ends:
        pairs.append((innov.at[pl.ds(first, REACH)], dst.at[:, pl.ds(0, members), :]))
    fetch(pairs, sems)
    for first, dst in ends:
        for b in range(REACH):
            number = jnp.full((1, CH), count[first + b].astype(F32))
            rest = jnp.zeros((4, CH), F32)
            dst[b, members:, :] = jnp.concatenate(
                [pos[first + b], sigma[first + b : first + b + 1, :], number, rest], axis=0
            )


def own_kernel(innov_in, pos_in, sigma_in, err_in, count_in, ev, od, vec, geo, acc, ints, floats,
               down, across, innov, pos, sigma, err, count, parts, col_x, col_y, sems):
    blocks = innov.shape[0]
    fetch(
        [(innov_in, innov), (pos_in, pos), (sigma_in, sigma), (err_in, err), (count_in, count)],
        sems,
    )
    acc[...] = jnp.zeros_like(acc)
    origin = pos[0, 0:1, 0:1]

    def pack(b, offset):
        number = count[b]
        ints[b] = offset
        pack_block(innov[b], number, offset, vec)
        pair = pos[b]
        rows = jnp.concatenate(
            [
                (pair[0:1] - origin) * UNIT,
                pair[1:2] * UNIT,
                sigma[pl.ds(b, 1), :],
                err[pl.ds(b, 1), :],
                jnp.zeros((4, CH), F32),
            ],
            axis=0,
        )
        pack_block(rows, number, offset, geo)
        return offset + number

    size = lax.fori_loop(0, blocks, pack, jnp.int32(0))
    ints[blocks] = size
    chunks = (size + CH - 1) // CH
    floats[0] = jnp.max(origin)

    def prepare(i, carry):
        where = at(i * CH)
        x = geo[0:1, where]
        col_x[i] = columns(x)
        col_y[i] = columns(geo[1:2, where])
        put_split(vec[:, where] * geo[2:3, where], parts, i)
        live = lanes((1, CH)) + i * CH < size
        floats[1 + i] = jnp.min(jnp.where(live, x, 3e38))
        floats[1 + blocks + i] = jnp.max(jnp.where(live, x, -3e38))
        return carry

    lax.fori_loop(0, chunks, prepare, 0)

    def enlist(i, t):
        end = floats[1 + blocks + i]
        for d in range(SPAN):
            j = i + d
            start = floats[1 + jnp.minimum(j, blocks - 1)]
            down[t] = i
            across[t] = j
            t = t + jnp.where((j < chunks) & (start - end < LIMIT), 1, 0)
        return t

    total = lax.fori_loop(0, chunks, enlist, jnp.int32(0))
    for extra in range(3):
        down[total + extra] = 0
        across[total + extra] = 0
    ints[blocks + 1] = total

    def make(t, ref, slot):
        where = at(across[t] * CH)
        build(col_x, col_y, down[t], geo[0:1, where], geo[1:2, where], ref, slot)

    make(0, ev, 0)

    def step(p, carry):
        t = 2 * p
        make(t + 1, od, p)
        own_product(t, total, down, across, parts, ev, p, acc)
        make(t + 2, ev, p + 1)
        own_product(t + 1, total, down, across, parts, od, p, acc)
        return carry

    lax.fori_loop(0, (total + 1) // 2, step, 0)


def edge_kernel(behind, ahead, vec, geo, acc, ints, floats, ev, od, side_geo, side_ints, down,
                across, out, parts, to_prev, to_next, side_vec, side_parts, col_x, col_y):
    members = vec.shape[0]
    blocks = (vec.shape[1] - 2 * CH) // CH
    wide = side_vec.shape[1] // 2
    size = ints[blocks]
    chunks = (size + CH - 1) // CH
    origin = floats[0]
    out[...] = jnp.zeros_like(out)
    side_ends = []
    for side, ref in enumerate((behind, ahead)):
        offset = jnp.int32(side * wide)
        for b in range(REACH):
            misc = ref[b, members:, :]
            number = misc[3, 0].astype(I32)
            pack_block(ref[b, :members, :], number, offset, side_vec)
            rows = jnp.concatenate(
                [(misc[0:1] - origin) * UNIT, misc[1:2] * UNIT, misc[2:]], axis=0
            )
            pack_block(rows, number, offset, side_geo)
            offset = offset + number
        side_ends.append(offset)
    total = jnp.int32(0)
    down[0] = 0
    across[0] = 0
    for side, end in enumerate(side_ends):
        begin = side * (wide // CH)
        side_chunks = (end - side * wide + CH - 1) // CH

        def prepare(h, t, begin=begin, end=end, side=side):
            place = begin + h
            where = at(place * CH)
            x = side_geo[0:1, where]
            col_x[place] = columns(x)
            col_y[place] = columns(side_geo[1:2, where])
            put_split(side_vec[:, where] * side_geo[2:3, where], side_parts, place)
            live = lanes((1, CH)) + place * CH < end
            if side == 0:
                edge = jnp.max(jnp.where(live, x, -3e38))
            else:
                edge = jnp.min(jnp.where(live, x, 3e38))
            for d in range(SPAN):
                if side == 0:
                    i = jnp.minimum(d, chunks - 1)
                    near = floats[1 + i] - edge < LIMIT
                else:
                    i = jnp.maximum(chunks - 1 - d, 0)
                    near = edge - floats[1 + blocks + i] < LIMIT
                down[t] = place
                across[t] = i
                t = t + jnp.where(near & (d < chunks), 1, 0)
            return t

        total = lax.fori_loop(0, side_chunks, prepare, total)
    last = jnp.maximum(total - 1, 0)
    for extra in range(3):
        down[total + extra] = down[last]
        across[total + extra] = across[last]
    side_ints[0] = total

    def make(t, ref, slot):
        where = at(across[t] * CH)
        build(col_x, col_y, down[t], geo[0:1, where], geo[1:2, where], ref, slot)

    make(0, ev, 0)

    def step(p, carry):
        t = 2 * p
        make(t + 1, od, p)
        edge_product(t, total, down, across, side_parts, ev, p, out)
        make(t + 2, ev, p + 1)
        edge_product(t + 1, total, down, across, side_parts, od, p, out)
        return carry

    lax.fori_loop(0, (total + 1) // 2, step, 0)

    def finish(i, carry):
        where = at(i * CH)
        scale = geo[2:3, where]
        image = scale * (out[:, where] + acc[:, where]) + geo[3:4, where] * vec[:, where]
        out[:, where] = image
        put_split(image * scale, parts, i)
        return carry

    lax.fori_loop(0, chunks, finish, 0)
    to_prev[...] = out[:, : REACH * CH]
    start = ints[blocks - REACH]
    base = (start // LN) * LN
    shift = start - base
    back = lax.rem(LN - shift, LN)
    keep = lanes((members, LN)) < LN - shift
    turned = pltpu.roll(out[:, at(base, LN)], back, 1)
    for k in range(REACH * CH // LN):
        following = pltpu.roll(out[:, at(base + (k + 1) * LN, LN)], back, 1)
        to_next[:, k * LN : (k + 1) * LN] = jnp.where(keep, turned, following)
        turned = following


def again_kernel(ev, od, parts, ints, down, across, acc):
    blocks = acc.shape[1] // CH - 2
    total = ints[blocks + 1]
    acc[...] = jnp.zeros_like(acc)

    def step(p, carry):
        t = 2 * p
        own_product(t, total, down, across, parts, ev, p, acc)
        own_product(t + 1, total, down, across, parts, od, p, acc)
        return carry

    lax.fori_loop(0, (total + 1) // 2, step, 0)


def lane_sum(values):
    return jnp.sum(values, axis=1, keepdims=True)


def last_kernel(behind, ahead, side_geo, side_ints, ev, od, down, across, acc, vec, image, geo,
                ints, out, sums, side_parts, total_ref):
    members = vec.shape[0]
    blocks = vec.shape[1] // CH - 2
    chunks = (ints[blocks] + CH - 1) // CH
    total = side_ints[0]
    total_ref[...] = acc[...]
    per_side = side_geo.shape[1] // CH // 2
    for side, ref in enumerate((behind, ahead)):
        for h in range(REACH):
            place = side * per_side + h
            scale = side_geo[2:3, place * CH : (place + 1) * CH]
            scaled = jnp.where(scale > 0, ref[:, h * CH : (h + 1) * CH] * scale, 0.0)
            put_split(scaled, side_parts, place)

    def step(p, carry):
        t = 2 * p
        edge_product(t, total, down, across, side_parts, ev, p, total_ref)
        edge_product(t + 1, total, down, across, side_parts, od, p, total_ref)
        return carry

    lax.fori_loop(0, (total + 1) // 2, step, 0)
    out[...] = jnp.zeros_like(out)
    zero = jnp.zeros((members, 1), F32)

    def first(i, carry):
        m0, m1 = carry
        where = at(i * CH)
        r, y = vec[:, where], image[:, where]
        out[:, where] = geo[2:3, where] * total_ref[:, where] + geo[3:4, where] * y
        return m0 + lane_sum(r * r), m1 + lane_sum(r * y)

    m0, m1 = lax.fori_loop(0, chunks, first, (zero, zero))
    mean = jnp.where(m0 > 0, m1 / jnp.where(m0 > 0, m0, 1.0), 0.0)

    def second(i, carry):
        vv, zu, cross, slip = carry
        where = at(i * CH)
        r, y = vec[:, where], image[:, where]
        z = y - mean * r
        u = out[:, where] - mean * y
        return (
            vv + lane_sum(z * z),
            zu + lane_sum(z * u),
            cross + lane_sum(z * y + r * u),
            slip + lane_sum(z * r),
        )

    found = lax.fori_loop(0, chunks, second, (zero, zero, zero, zero))
    table = jnp.zeros((members, LN), F32)
    lane = lanes((members, LN))
    for k, value in enumerate((m0, m1, mean) + tuple(found)):
        table = jnp.where(lane == k, value, table)
    turned = jnp.concatenate([table, jnp.zeros((LN - members, LN), F32)], axis=0).T[:8]
    for k in range(sums.shape[0]):
        sums[k] = turned


def update_kernel(sums, vec, image, second, ints, count, solution_ref, residual_ref, packed):
    members = vec.shape[0]
    blocks = vec.shape[1] // CH - 2
    chunks = (ints[blocks] + CH - 1) // CH
    terms = sums[...]
    m0 = jnp.sum(terms[:, 0, :], axis=0, keepdims=True)
    m1 = jnp.sum(terms[:, 1, :], axis=0, keepdims=True)
    used = lanes((1, LN)) < members
    m0 = jnp.where(used, m0, 1.0)
    m1 = jnp.where(used, m1, 1.0)
    mean = m1 / m0
    off = mean - terms[:, 2, :]
    vv = terms[:, 3, :] - 2.0 * off * terms[:, 6, :] + off * off * terms[:, 0, :]
    zu = terms[:, 4, :] - off * terms[:, 5, :] + off * off * terms[:, 1, :]
    cross = terms[:, 5, :] - 2.0 * off * terms[:, 1, :]
    vv, zu, cross = (jnp.sum(x, axis=0, keepdims=True) for x in (vv, zu, cross))
    alpha = m0 / m1
    rr = alpha * alpha * vv
    beta = rr / m0
    alpha_next = rr / (alpha * alpha * zu - alpha * beta * cross + beta * beta * m1)
    one = alpha + alpha_next * (1.0 + beta)
    two = alpha * alpha_next
    table = jnp.concatenate([one, two, jnp.zeros((LN - 2, LN), F32)], axis=0).T
    one, two = table[:members, 0:1], table[:members, 1:2]

    packed[...] = jnp.zeros_like(packed)

    def combine(i, carry):
        where = at(i * CH)
        r, y, yy = vec[:, where], image[:, where], second[:, where]
        packed[:members, where] = one * r - two * y
        packed[members:, where] = r - one * y + two * yy
        return carry

    lax.fori_loop(0, chunks, combine, 0)

    def unpack(b, carry):
        offset, number = ints[b], count[b]
        base = (offset // LN) * LN
        shift = offset - base
        back = lax.rem(LN - shift, LN)
        lane = lanes((2 * members, LN))
        keep = lane < LN - shift
        turned = [pltpu.roll(packed[:, at(base + k * LN, LN)], back, 1) for k in range(3)]
        for k in range(2):
            part = jnp.where(keep, turned[k], turned[k + 1])
            part = jnp.where(lane + k * LN < number, part, 0.0)
            solution_ref[b, :, k * LN : (k + 1) * LN] = part[:members]
            residual_ref[b, :, k * LN : (k + 1) * LN] = part[members:]
        return carry

    lax.fori_loop(0, blocks, unpack, 0)


def shift_by(block, distance):
    devices = range(lax.axis_size("region"))
    route = [(i, i + distance) for i in devices if i + distance in devices]
    return lax.ppermute(block, "region", route)


def call(kernel, name, in_specs, outs, scratch=(), limit=9 * MB, cost=None):
    return pl.pallas_call(
        kernel,
        name=name,
        in_specs=in_specs,
        out_specs=[spec for spec, _ in outs],
        out_shape=[shape for _, shape in outs],
        scratch_shapes=list(scratch),
        compiler_params=pltpu.CompilerParams(vmem_limit_bytes=limit),
        cost_estimate=cost,
    )


def body(obs_pos, obs_sigma, obs_error, innovation, obs_count, pair_list, pair_live):
    blocks, members, _ = innovation.shape
    sd = jax.ShapeDtypeStruct
    in_hbm = functools.partial(pltpu.with_memory_space_constraint, memory_space=pltpu.HBM)
    in_vmem = functools.partial(pltpu.with_memory_space_constraint, memory_space=pltpu.VMEM)
    wide = blocks * CH + 2 * CH
    side_chunks = REACH + 2
    own_tiles = (blocks * SPAN - SPAN * (SPAN - 1) // 2) // 2 + 3
    side_tiles = 2 * 25 // 2 + 3
    listed = 2 * own_tiles + 16
    pack_out = (VM, sd((REACH, members + 8, CH), F32))
    to_prev, to_next = call(
        pack_sides, "pack", [HB] * 4, [pack_out, pack_out],
        [
            pltpu.VMEM(obs_pos.shape, F32),
            pltpu.VMEM(obs_sigma.shape, F32),
            pltpu.SMEM(obs_count.shape, I32),
            pltpu.SemaphoreType.DMA((5,)),
        ],
        limit=3 * MB,
    )(*map(in_hbm, (innovation, obs_pos, obs_sigma, obs_count)))
    ahead = shift_by(to_prev, -1)
    behind = shift_by(to_next, 1)
    dense = (VM, sd((members, wide), F32))
    tile = (2 * CH, CH)
    ev, od, vec, geo, acc, ints, floats, down, across = call(
        own_kernel, "own", [HB] * 5,
        [
            (VM, pltpu.VMEM((own_tiles,) + tile, BF16)),
            (VM, pltpu.VMEM((own_tiles,) + tile, BF16)),
            dense,
            (VM, sd((8, wide), F32)),
            dense,
            (SM, sd((blocks + 2,), I32)),
            (SM, sd((2 * blocks + 1,), F32)),
            (SM, sd((listed,), I32)),
            (SM, sd((listed,), I32)),
        ],
        [
            pltpu.VMEM(innovation.shape, F32),
            pltpu.VMEM(obs_pos.shape, F32),
            pltpu.VMEM(obs_sigma.shape, F32),
            pltpu.VMEM(obs_error.shape, F32),
            pltpu.SMEM(obs_count.shape, I32),
            pltpu.VMEM((blocks, 2 * members, CH), BF16),
            pltpu.VMEM((blocks, CH, LN), F32),
            pltpu.VMEM((blocks, CH, LN), F32),
            pltpu.SemaphoreType.DMA((5,)),
        ],
        cost=pl.CostEstimate(flops=4 * 10**9, bytes_accessed=20 * MB, transcendentals=0),
    )(*map(in_hbm, (innovation, obs_pos, obs_sigma, obs_error, obs_count)))
    ev, od = in_vmem(ev), in_vmem(od)
    side = (VM, sd((members, REACH * CH), F32))
    (side_ev, side_od, side_geo, side_ints, side_down, side_across, image, parts, image_prev,
     image_next) = call(
        edge_kernel, "edge", [VM, VM, VM, VM, VM, SM, SM],
        [
            (VM, pltpu.VMEM((side_tiles,) + tile, BF16)),
            (VM, pltpu.VMEM((side_tiles,) + tile, BF16)),
            (VM, sd((8, 2 * side_chunks * CH), F32)),
            (SM, sd((1,), I32)),
            (SM, sd((128,), I32)),
            (SM, sd((128,), I32)),
            dense,
            (VM, sd((blocks, 2 * members, CH), BF16)),
            side,
            side,
        ],
        [
            pltpu.VMEM((members, 2 * side_chunks * CH), F32),
            pltpu.VMEM((2 * side_chunks, 2 * members, CH), BF16),
            pltpu.VMEM((2 * side_chunks, CH, LN), F32),
            pltpu.VMEM((2 * side_chunks, CH, LN), F32),
        ],
        limit=7 * MB,
    )(behind, ahead, vec, geo, acc, ints, floats)
    side_ev, side_od = in_vmem(side_ev), in_vmem(side_od)
    image_ahead = shift_by(image_prev, -1)
    image_behind = shift_by(image_next, 1)
    (acc,) = call(
        again_kernel, "again", [VM, VM, VM, SM, SM, SM], [dense], limit=2 * MB,
        cost=pl.CostEstimate(flops=4 * 10**9, bytes_accessed=20 * MB, transcendentals=0),
    )(ev, od, parts, ints, down, across)
    devices = lax.axis_size("region")
    second, sums = call(
        last_kernel, "last", [VM, VM, VM, SM, VM, VM, SM, SM, VM, VM, VM, VM, SM],
        [dense, (VM, sd((devices, 8, LN), F32))],
        [
            pltpu.VMEM((2 * side_chunks, 2 * members, CH), BF16),
            pltpu.VMEM((members, wide), F32),
        ],
        limit=4 * MB,
    )(image_behind, image_ahead, side_geo, side_ints, side_ev, side_od, side_down, side_across,
      acc, vec, image, geo, ints)
    sums = lax.all_to_all(sums, "region", 0, 0)
    field = (VM, sd((blocks, members, CH), F32))
    return tuple(call(
        update_kernel, "update", [VM, VM, VM, VM, SM, SM], [field, field],
        [pltpu.VMEM((2 * members, wide), F32)],
        limit=6 * MB,
    )(sums, vec, image, second, ints, obs_count))


def solution(mesh):
    return jax.shard_map(
        body,
        mesh=mesh,
        in_specs=(
            P(("groups", "region"), None, None),
            P(("groups", "region"), None),
            P(("groups", "region"), None),
            P(("groups", "region"), None, None),
            P(("groups", "region")),
            P(None, ("groups", "region")),
            P(("groups", "region")),
        ),
        out_specs=(P(("groups", "region"), None, None), P(("groups", "region"), None, None)),
        check_vma=False,
    )
```

time: 528 us -> 71.9 us (0.14); the launches traced: 519 us -> 72.7 us
  matrix products: 238 us -> 0 us
  local copies, waits for them, and re-layouts: 110 us -> 6.18 us
  blocking collectives: 98.6 us -> 22.6 us
  other arithmetic: 42.3 us -> 0 us
  Pallas kernels: 0 us -> 26.7 us
  starting transfers between devices: 21.2 us -> 11.7 us
    dot_general x36 -> x0, matrix products: 238 us -> none  [the longest x16 109 us: group_terms(): jnp.einsum('pab,pmb->pma', tiles, jnp.take(dir_window, second_part, axis=...]
    psum x3 -> x0, blocking collectives: 98.6 us -> none  [the longest x2 64.5 us: squares(): return lax.psum(member_sum(residual * residual), 'region')]
    gather x64 -> x0, local copies, waits for them, and re-layouts: 68.9 us -> none  [the longest x16 17.6 us: group_terms(): jnp.take(dir_window, first_part, axis=0)]
    pallas_call x0 -> x6, Pallas kernels: none -> 26.7 us  [the longest x1 10.7 us: body(): call(own_kernel, 'own', [HB] * 5, [(VM, pltpu.VMEM((own_tiles,) + tile, B...]
    all_to_all x0 -> x1, blocking collectives: none -> 22.6 us  [body(): sums = lax.all_to_all(sums, 'region', 0, 0)]
    while x162 -> x0, local copies, waits for them, and re-layouts: 20.5 us -> none
    and x16 -> x0, other arithmetic: 15.3 us -> none  [group_terms(): jnp.take(geo_window, first_part, axis=0)]
    another operation x4 -> x0, local copies, waits for them, and re-layouts: 13.7 us -> none
  transfers between devices with their start and end apart: 5 -> 4, of which waited for: 4 -> 1; matrix products, arithmetic and copies ran while one was open for 0% -> 0% of each run, Pallas kernels for 0% -> 20%
where the time goes in v1:
time: 71.9 us; the launch traced here: 72.7 us
  Pallas kernels  26.7 us (37%)
  blocking collectives  22.6 us (31%)
  starting transfers between devices  11.7 us (16%)
  local copies, waits for them, and re-layouts  6.18 us (9%)
  waiting for transfers between devices  4.82 us (7%)
  between operations  0.75 us (1%)
    all_to_all x1, blocking collectives, body(): sums = lax.all_to_all(sums, 'region', 0, 0)  22.6 us
    ppermute x4, starting transfers between devices, shift_by(): return lax.ppermute(block, 'region', route)  11.7 us
    pallas_call x1, Pallas kernels, body(): call(own_kernel, 'own', [HB] * 5, [(VM, pltpu.VMEM((own_tiles,) + tile, B...  10.7 us
    unnamed x10, local copies, waits for them, and re-layouts  6.18 us
    ppermute x4, waiting for transfers between devices, shift_by(): return lax.ppermute(block, 'region', route)  4.82 us
    pallas_call x1, Pallas kernels, body(): call(update_kernel, 'update', [VM, VM, VM, VM, SM, SM], [field, field], [...  4.73 us
    pallas_call x1, Pallas kernels, body(): call(again_kernel, 'again', [VM, VM, VM, SM, SM, SM], [dense], limit=2 *...  3.99 us
    pallas_call x1, Pallas kernels, body(): call(last_kernel, 'last', [VM, VM, VM, SM, VM, VM, SM, SM, VM, VM, VM, VM...  3.32 us
  transfers between devices with their start and end apart: 4, of which 1 were waited for; matrix products, arithmetic and copies ran while one was open for 0% of the time, Pallas kernels for 20%

profile of v1, /device:TPU:0, one launch (start us, length us, event | category | flops | bytes accessed | tf_op | source)
XLA Modules:
  0.0 72.7 jit_solution(7656693040844299187)
XLA Ops:
  0.6 1.2 %pack.1 = (f32[5,72,256]{2,1,0:T(8,128)S(1)}, f32[5,72,256]{2,1,0:T(8,128)S(1)}) custom-call(f32[16,64,256]{2,1,0:T(8,128)} %innov_in.1, f32[16,2,256]{2,1,0:T(2,128)} %pos_in.3, f32[16,256]{1,0:T(8,128)} %sigma_in.3, s32[16]{0:T(128)} %count.1), custom_call_target="tpu_custom_call" | custom-call | tf_op jit(solution)/shard_map/pack/pallas_call | solution.py:466
  1.8 2.4 %collective-permute-start = (f32[5,72,256]{2,1,0:T(8,128)S(1)}, f32[5,72,256]{2,1,0:T(8,128)S(1)}, u32[]{:S(2)}, u32[]{:S(2)}) collective-permute-start(f32[5,72,256]{2,1,0:T(8,128)S(1)} %get-tuple-element.25), channel_id=1, source_target_pairs={{0,1},{1,2},{2,3},{3,4},{4,5},{5,6},{6,7},{7,8},{8,9},{9,10},{10,1... | collective-permute-start | bytes 1105928 | tf_op jit(solution)/shard_map/ppermute | solution.py:439
  4.2 1.3 %collective-permute-start.1 = (f32[5,72,256]{2,1,0:T(8,128)S(1)}, f32[5,72,256]{2,1,0:T(8,128)S(1)}, u32[]{:S(2)}, u32[]{:S(2)}) collective-permute-start(f32[5,72,256]{2,1,0:T(8,128)S(1)} %get-tuple-element.26), channel_id=1, source_target_pairs={{1,0},{2,1},{3,2},{4,3},{5,4},{6,5},{7,6},{8,7},{9,8},{10,9},{11,1... | collective-permute-start | bytes 1105928 | tf_op jit(solution)/shard_map/ppermute | solution.py:439
  5.5 10.7 %own.1 = (bf16[48,512,256]{2,1,0:T(8,128)(2,1)S(1)}, bf16[48,512,256]{2,1,0:T(8,128)(2,1)S(1)}, f32[64,4608]{1,0:T(8,128)S(1)}, f32[8,4608]{1,0:T(8,128)S(1)}, f...) custom-call(f32[16,64,256]{2,1,0:T(8,128)} %innov_in.1, ...), custom_call_target="tpu_custom_call" | custom-call | flops 4000000000 | bytes 20971520 | tf_op jit(solution)/shard_map/own/pallas_call | solution.py:480
  16.2 0.0 collective-permute-done.behind
  16.2 0.0 collective-permute-done.1.ahead
  16.2 2.8 %edge.1 = (bf16[28,512,256]{2,1,0:T(8,128)(2,1)S(1)}, bf16[28,512,256]{2,1,0:T(8,128)(2,1)S(1)}, f32[8,3584]{1,0:T(8,128)S(1)}, s32[1]{0:T(128)}, s32[128]{0:T(1...) custom-call(f32[5,72,256]{2,1,0:T(8,128)S(1)} %collective-permute-do, ...), custom_call_target="tpu_custom_call" | custom-call | tf_op jit(solution)/shard_map/edge/pallas_call | solution.py:509
  19.0 0.0 copy-start
  19.0 0.0 copy-start.2
  19.0 6.7 %collective-permute-start.2 = (f32[64,1280]{1,0:T(8,128)S(1)}, f32[64,1280]{1,0:T(8,128)S(1)}, u32[]{:S(2)}, u32[]{:S(2)}) collective-permute-start(f32[64,1280]{1,0:T(8,128)S(1)} %get-tuple-element.32), channel_id=1, source_target_pairs={{0,1},{1,2},{2,3},{3,4},{4,5},{5,6},{6,7},{7,8},{8,9},{9,10},{10,1... | collective-permute-start | bytes 983048 | tf_op jit(solution)/shard_map/ppermute | solution.py:439
  25.7 1.3 %collective-permute-start.3 = (f32[64,1280]{1,0:T(8,128)S(1)}, f32[64,1280]{1,0:T(8,128)S(1)}, u32[]{:S(2)}, u32[]{:S(2)}) collective-permute-start(f32[64,1280]{1,0:T(8,128)S(1)} %get-tuple-element.33), channel_id=1, source_target_pairs={{1,0},{2,1},{3,2},{4,3},{5,4},{6,5},{7,6},{8,7},{9,8},{10,9},{11,1... | collective-permute-start | bytes 983048 | tf_op jit(solution)/shard_map/ppermute | solution.py:439
  27.0 4.0 %again.1.acc = f32[64,4608]{1,0:T(8,128)S(1)} custom-call(bf16[48,512,256]{2,1,0:T(8,128)(2,1)S(1)} %get-tuple-element.40.ev, bf16[48,512,256]{2,1,0:T(8,128)(2,1)S(1)} %get-tuple-element.41.od, bf16[16,128,256]{2,1,0:T(8,128)(2,1)S(1)} %get-tuple-element.42.parts, s32[18]{0:T(128)S(1)} %get-tuple-element.30.ints, s32[112]{0:T(128)S(1)} %get-tuple-element.43.down, ...), custom_call_target="tpu_custom_call" | custom-call | flops 4000000000 | bytes 20971520 | tf_op jit(solution)/shard_map/again/pallas_call | solution.py:534
  31.0 0.0 copy-done
  31.0 0.0 copy-done.2
  31.0 0.0 collective-permute-done.2.behind
  31.1 4.8 %collective-permute-done.3.ahead = f32[64,1280]{1,0:T(8,128)S(1)} collective-permute-done((f32[64,1280]{1,0:T(8,128)S(1)}, f32[64,1280]{1,0:T(8,128)S(1)}, u32[]{:S(2)}, u32[]{:S(2)}) %collective-permute-start.3) | collective-permute-done | bytes 327712 | tf_op jit(solution)/shard_map/ppermute | solution.py:439
  35.9 0.0 copy-start.1
  35.9 3.1 %copy-done.1 = bf16[28,512,256]{2,1,0:T(8,128)(2,1)S(1)} copy-done((bf16[28,512,256]{2,1,0:T(8,128)(2,1)S(1)}, bf16[28,512,256]{2,1,0:T(8,128)(2,1)}, u32[]{:S(2)}) %copy-start.1) | copy-done | bytes 7340056
  38.9 0.0 copy-start.3
  38.9 3.1 %copy-done.3 = bf16[28,512,256]{2,1,0:T(8,128)(2,1)S(1)} copy-done((bf16[28,512,256]{2,1,0:T(8,128)(2,1)S(1)}, bf16[28,512,256]{2,1,0:T(8,128)(2,1)}, u32[]{:S(2)}) %copy-start.3) | copy-done | bytes 7340056
  42.0 0.0 copy-start.4
  42.0 3.3 %last.1 = (f32[64,4608]{1,0:T(8,128)S(1)}, f32[16,8,128]{2,1,0:T(8,128)S(1)}) custom-call(f32[64,1280]{1,0:T(8,128)S(1)} %collective-permute-done.2.behind, f32[64,1280]{1,0:T(8,128)S(1)} %collective-permute-done.3.ahead, f32[8,3584]{1,0:T(8,128)S(1)} %get-tuple-element.34.side_geo, s32[1]{0:T(128)} %get-tuple-element.35.side_ints, ...), custom_call_target="tpu_custom_call" | custom-call | tf_op jit(solution)/shard_map/last/pallas_call | solution.py:539
  45.4 22.6 %all_to_all.5.sums = f32[16,8,128]{2,1,0:T(8,128)S(1)} all-to-all(f32[16,8,128]{2,1,0:T(8,128)S(1)} %get-tuple-element.46), channel_id=1, replica_groups=mesh['groups'=2,'region'=16] {'region'}, dimensions={0} | all-to-all | bytes 131072 | tf_op jit(solution)/shard_map/all_to_all | solution.py:549
  68.0 0.0 copy-done.4
  68.0 4.7 %update.1 = (f32[16,64,256]{2,1,0:T(8,128)}, f32[16,64,256]{2,1,0:T(8,128)}) custom-call(f32[16,8,128]{2,1,0:T(8,128)S(1)} %all_to_all.5.sums, f32[64,4608]{1,0:T(8,128)S(1)} %get-tuple-element.27.vec, f32[64,4608]{1,0:T(8,128)S(1)} %get-tuple-element.45.image, f32[64,4608]{1,0:T(8,128)S(1)} %get-tuple-element.47.second, s32[18]{0:T(128)S(1)} %get-tuple-element.30.ints, ...), custom_call_target="tpu_custom_call" | custom-call | tf_op jit(solution)/shard_map/update/pallas_call | solution.py:551
Async XLA Ops:
  1.8 14.4 %collective-permute-start = (f32[5,72,256]{2,1,0:T(8,128)S(1)}, f32[5,72,256]{2,1,0:T(8,128)S(1)}, u32[]{:S(2)}, u32[]{:S(2)}) collective-permute-start(f32[5,72,256]{2,1,0:T(8,128)S(1)} %get-tuple-element.25), channel_id=1, source_target_pairs={{0,1},{1,2},{2,3},{3,4},{4,5},{5,6},{6,7},{7,8},{8,9},{9,10},{10,1... | collective-permute-start | bytes 1105928 | tf_op jit(solution)/shard_map/ppermute | solution.py:439
  4.2 12.0 %collective-permute-start.1 = (f32[5,72,256]{2,1,0:T(8,128)S(1)}, f32[5,72,256]{2,1,0:T(8,128)S(1)}, u32[]{:S(2)}, u32[]{:S(2)}) collective-permute-start(f32[5,72,256]{2,1,0:T(8,128)S(1)} %get-tuple-element.26), channel_id=1, source_target_pairs={{1,0},{2,1},{3,2},{4,3},{5,4},{6,5},{7,6},{8,7},{9,8},{10,9},{11,1... | collective-permute-start | bytes 1105928 | tf_op jit(solution)/shard_map/ppermute | solution.py:439
  19.0 12.0 %copy-start = (bf16[28,512,256]{2,1,0:T(8,128)(2,1)}, bf16[28,512,256]{2,1,0:T(8,128)(2,1)S(1)}, u32[]{:S(2)}) copy-start(bf16[28,512,256]{2,1,0:T(8,128)(2,1)S(1)} %get-tuple-element.36.ev) | copy-start | bytes 22020100
  19.0 12.0 %copy-start.2 = (bf16[28,512,256]{2,1,0:T(8,128)(2,1)}, bf16[28,512,256]{2,1,0:T(8,128)(2,1)S(1)}, u32[]{:S(2)}) copy-start(bf16[28,512,256]{2,1,0:T(8,128)(2,1)S(1)} %get-tuple-element.37.od) | copy-start | bytes 22020100
  19.0 12.0 %collective-permute-start.2 = (f32[64,1280]{1,0:T(8,128)S(1)}, f32[64,1280]{1,0:T(8,128)S(1)}, u32[]{:S(2)}, u32[]{:S(2)}) collective-permute-start(f32[64,1280]{1,0:T(8,128)S(1)} %get-tuple-element.32), channel_id=1, source_target_pairs={{0,1},{1,2},{2,3},{3,4},{4,5},{5,6},{6,7},{7,8},{8,9},{9,10},{10,1... | collective-permute-start | bytes 983048 | tf_op jit(solution)/shard_map/ppermute | solution.py:439
  25.7 10.1 %collective-permute-start.3 = (f32[64,1280]{1,0:T(8,128)S(1)}, f32[64,1280]{1,0:T(8,128)S(1)}, u32[]{:S(2)}, u32[]{:S(2)}) collective-permute-start(f32[64,1280]{1,0:T(8,128)S(1)} %get-tuple-element.33), channel_id=1, source_target_pairs={{1,0},{2,1},{3,2},{4,3},{5,4},{6,5},{7,6},{8,7},{9,8},{10,9},{11,1... | collective-permute-start | bytes 983048 | tf_op jit(solution)/shard_map/ppermute | solution.py:439
  35.9 3.1 %copy-start.1 = (bf16[28,512,256]{2,1,0:T(8,128)(2,1)S(1)}, bf16[28,512,256]{2,1,0:T(8,128)(2,1)}, u32[]{:S(2)}) copy-start(bf16[28,512,256]{2,1,0:T(8,128)(2,1)} %copy-done) | copy-start | bytes 22020100
  38.9 3.1 %copy-start.3 = (bf16[28,512,256]{2,1,0:T(8,128)(2,1)S(1)}, bf16[28,512,256]{2,1,0:T(8,128)(2,1)}, u32[]{:S(2)}) copy-start(bf16[28,512,256]{2,1,0:T(8,128)(2,1)} %copy-done.2) | copy-start | bytes 22020100
  42.0 25.9 %copy-start.4 = (s32[16]{0:T(128)S(1)}, s32[16]{0:T(128)}, u32[]{:S(2)}) copy-start(s32[16]{0:T(128)} %count.1) | copy-start | bytes 196
